TPU v7x, 32 devices: a whole 2x2x4 slice. The times are simulated.
32 devices in a mesh: clip: 2 (over x), bank: 16 (over z, y, core).
Axes of the slice: x: 2, y: 2, z: 4, core: 2. Of those that a mesh axis runs over, the one named last changes fastest.
Arguments:
- queries: bfloat16 [2, 256, 1536], P('clip', 'bank'), may hold values from -120 to 120
- keys: bfloat16 [2, 2048, 1536], P('clip', 'bank'), may hold values from -6 to 6
- values: bfloat16 [2, 2048, 1536], P('clip', 'bank'), may hold values from -6 to 6
- grad_out: bfloat16 [2, 256, 1536], P('clip', 'bank'), may hold values from -6 to 6
- null_key: bfloat16 [1536], replicated, may hold values from -4 to 4
- null_value: bfloat16 [1536], replicated, may hold values from -4 to 4
- bank_counts: int32 [2], P('clip'), may hold values from 128 to 2048, as said below
- block_slot: int32 [2, 16], P('clip', 'bank'), may hold values from 0 to 15, each once within a row
Outputs:
- grad_queries: bfloat16 [2, 256, 1536], P('clip', 'bank')
- grad_keys: bfloat16 [2, 2048, 1536], P('clip', 'bank')
- grad_values: bfloat16 [2, 2048, 1536], P('clip', 'bank')
- grad_null_key: float32 [1536], replicated
- grad_null_value: float32 [1536], replicated
Inputs may be any that keep to these rules, and one draw needn't show every extreme that they name: `bank_counts`: a multiple of 128; exactly one group holds 2048 live tokens. `block_slot`: each row is a permutation of the device indices.
All inputs are finite; a program needn't handle non-finite values.
Results may differ from a plain program's by a relative error of at most 0.01155.
Values may be sent and summed in bfloat16 or wider, within the bound.
A program may use at most 64 MiB of HBM per device.

v0:
```python
import functools

import jax
import jax.numpy as jnp
from jax import lax
from jax.experimental import pallas as pl
from jax.experimental.pallas import tpu as pltpu
from jax.sharding import PartitionSpec as P

HEADS = 12
HD = 128
HW = HEADS * HD
SCALE = HD ** (-0.5)
F32 = jnp.float32
BF16 = jnp.bfloat16
PARTS = 3
PER = HEADS // PARTS
WIDE = PER * HD
NT = (((1,), (1,)), ((), ()))
TN = (((0,), (0,)), ((), ()))


def nt_dot(a, b):
    return lax.dot_general(a, b, NT, preferred_element_type=F32)


def halves(x):
    high = x.astype(BF16)
    return high, (x - high.astype(F32)).astype(BF16)


def merge(lses, deltas):
    top = functools.reduce(jnp.maximum, lses)
    weights = [jnp.exp(one - top) for one in lses]
    total = sum(weights[1:], weights[0])
    mixed = weights[0] * deltas[0]
    for weight, delta in zip(weights[1:], deltas[1:]):
        mixed = mixed + weight * delta
    return top + jnp.log(total), mixed / total


def kernel(
    n_clip, n_z, rows, blk,
    valid_ref, q_hbm, k_hbm, v_hbm, do_hbm, nk_hbm, nv_hbm,
    gq_ref, gk_hbm, gv_hbm, gn_ref,
    q_all, do_all, e_s, dp_s, p_s, ds_s, dq_s, dq_out, rs_c, y_out, rs_y, acc_s, z_out, rs_z,
    peak_s, st_lo, st_z, null_s, null_sums,
    k_ref, v_ref, nk_ref, nv_ref, gk_ref, gv_ref, load_sem,
    g_recv, g_recv_c, g_send_z, g_send_y, g_send_c, st_send, st_recv, rs_send, rs_recv, n_send, n_recv,
):
    n = 4 * n_z
    qt = n * rows
    clip = lax.axis_index("clip")
    bank = lax.axis_index("bank")
    core = lax.rem(bank, 2)
    y = lax.rem(bank // 2, 2)
    z = bank // 4

    def dev(z_, y_, c_):
        return (clip, (z_ * 2 + y_) * 2 + c_)

    def place(z_, y_, c_):
        return (c_ * 2 + y_) * n_z + z_

    mine = place(z, y, core)
    others_z = [lax.rem(z + j, n_z) for j in range(1, n_z)]
    lo_peers = [(y, 1 - core), (1 - y, core), (1 - y, 1 - core)]
    to_core, to_y = dev(z, y, 1 - core), dev(z, 1 - y, core)
    clip_peers = [lax.rem(clip + j, n_clip) for j in range(1, n_clip)]

    loads = [
        pltpu.make_async_copy(src, dst, load_sem.at[i])
        for i, (src, dst) in enumerate(
            [
                (q_hbm, q_all.at[mine]), (do_hbm, do_all.at[mine]), (k_hbm, k_ref), (v_hbm, v_ref),
                (nk_hbm, nk_ref), (nv_hbm, nv_ref),
            ]
        )
    ]
    for load in loads:
        load.start()

    barrier = pltpu.get_barrier_semaphore()
    peers = [dev(z, a, b) for a, b in lo_peers] + [dev(o, y, core) for o in others_z]
    peers += [(o, bank) for o in clip_peers]
    for peer in peers:
        pl.semaphore_signal(barrier, inc=1, device_id=peer, device_id_type=pl.DeviceIdType.MESH)
    pl.semaphore_wait(barrier, len(peers))

    def remote(src, dst, send, recv, device):
        copy = pltpu.make_async_remote_copy(
            src_ref=src, dst_ref=dst, send_sem=send, recv_sem=recv,
            device_id=device, device_id_type=pl.DeviceIdType.MESH,
        )
        copy.start()
        return copy

    gathered = (q_all, do_all)
    sends = []

    def own_sends(a):
        own = gathered[a].at[mine]
        for j, o in enumerate(others_z):
            sends.append(remote(own, own, g_send_z.at[a, j], g_recv.at[a, mine], dev(o, y, core)))
        sends.append(remote(own, own, g_send_y.at[a, 0], g_recv.at[a, mine], to_y))

    def landed(buf, send, recv):
        pltpu.make_async_remote_copy(
            src_ref=buf, dst_ref=buf, send_sem=send, recv_sem=recv,
            device_id=to_core, device_id_type=pl.DeviceIdType.MESH,
        ).wait_recv()

    def slab(a, y_, c_):
        return gathered[a].at[pl.ds(place(0, y_, c_), n_z)]

    def to_other_core(a, y_):
        here = slab(a, y_, core)
        sends.append(remote(here, here, g_send_c.at[a, y_], g_recv_c.at[a, y_], to_core))

    def forward(a, step):
        if step < n_z - 1:
            at = place(others_z[step], y, core)
            here = gathered[a].at[at]
            landed(here, g_send_z.at[a, 0], g_recv.at[a, at])
            sends.append(remote(here, here, g_send_y.at[a, step + 1], g_recv.at[a, at], to_y))
            if step == n_z - 2:
                to_other_core(a, y)
        else:
            at = place(([z] + others_z)[step - (n_z - 1)], 1 - y, core)
            landed(gathered[a].at[at], g_send_z.at[a, 0], g_recv.at[a, at])
            if step == 2 * n_z - 2:
                to_other_core(a, 1 - y)

    def from_core(a):
        for y_ in (y, 1 - y):
            landed(slab(a, y_, 1 - core), g_send_c.at[a, 0], g_recv_c.at[a, y_])

    loads[0].wait()
    own_sends(0)
    loads[1].wait()
    own_sends(1)
    steps = 2 * n_z - 1
    for step in range(steps):
        forward(0, step)
    loads[2].wait()
    from_core(0)

    live = lax.broadcasted_iota(jnp.int32, (blk, qt), 0) < valid_ref[0, 0]
    lo = core * 2 + y

    def cols(h):
        return slice(h * HD, (h + 1) * HD)

    def head_of(ref, h):
        return ref[:, :, cols(h)].reshape(qt, HD)

    totals = []
    done = 0
    for h in range(HEADS):
        until = min(steps, (steps * max(h - 1, 0) + 8) // 9)
        for step in range(done, until):
            forward(1, step)
        done = max(done, until)
        scores = nt_dot(k_ref[:, cols(h)], head_of(q_all, h)) * SCALE
        scores = jnp.where(live, scores, -1e30)
        peak = jnp.max(scores, axis=0, keepdims=True)
        e = jnp.exp(scores - peak)
        total = jnp.sum(e, axis=0, keepdims=True)
        e_s[h] = e
        peak_s[h : h + 1, :] = peak
        st_lo[lo, h : h + 1, :] = peak + jnp.log(total)
        totals.append(total)
    for step in range(done, steps):
        forward(1, step)
    loads[3].wait()
    from_core(1)
    for h in range(HEADS):
        dp = nt_dot(v_ref[:, cols(h)], head_of(do_all, h))
        dp_s[h] = dp
        st_lo[lo, HEADS + h : HEADS + h + 1, :] = jnp.sum(e_s[h] * dp, axis=0, keepdims=True) / totals[h]

    st = [
        remote(st_lo.at[lo], st_lo.at[lo], st_send.at[0, i], st_recv.at[0, lo], dev(z, a, b))
        for i, (a, b) in enumerate(lo_peers)
    ]
    loads[4].wait()
    loads[5].wait()
    row_of = lax.broadcasted_iota(jnp.int32, (16, HW), 0)
    col_of = lax.broadcasted_iota(jnp.int32, (16, HW), 1)
    diagonal = (col_of >= row_of * HD) & (col_of < (row_of + 1) * HD)
    nk_diag = jnp.where(diagonal, jnp.broadcast_to(nk_ref[...].astype(F32).reshape(1, HW), (16, HW)), 0.0).astype(BF16)
    nv_diag = jnp.where(diagonal, jnp.broadcast_to(nv_ref[...].astype(F32).reshape(1, HW), (16, HW)), 0.0).astype(BF16)
    whole_q = q_all[...].reshape(qt, HW)
    whole_do = do_all[...].reshape(qt, HW)
    null_score = (nt_dot(nk_diag, whole_q) * SCALE)[:HEADS]
    null_dp = nt_dot(nv_diag, whole_do)[:HEADS]

    def stat_arrived(stage, buf, at):
        pltpu.make_async_remote_copy(
            src_ref=buf.at[at], dst_ref=buf.at[at], send_sem=st_send.at[stage, 0], recv_sem=st_recv.at[stage, at],
            device_id=to_core, device_id_type=pl.DeviceIdType.MESH,
        ).wait_recv()

    for a, b in lo_peers:
        stat_arrived(0, st_lo, b * 2 + a)
    lse, delta = merge([st_lo[i, :HEADS] for i in range(4)], [st_lo[i, HEADS:] for i in range(4)])
    st_z[z, :HEADS, :] = lse
    st_z[z, HEADS:, :] = delta
    for j, o in enumerate(others_z):
        st.append(remote(st_z.at[z], st_z.at[z], st_send.at[1, j], st_recv.at[1, z], dev(o, y, core)))
    for o in others_z:
        stat_arrived(1, st_z, o)
    lse, delta = merge([st_z[i, :HEADS] for i in range(n_z)], [st_z[i, HEADS:] for i in range(n_z)])
    top = jnp.maximum(lse, null_score)
    log_total = top + jnp.log(jnp.exp(lse - top) + jnp.exp(null_score - top))
    null_prob = jnp.exp(null_score - log_total)
    delta = jnp.exp(lse - log_total) * delta + null_prob * null_dp
    null_ds = null_prob * (null_dp - delta)
    factor = jnp.exp(peak_s[:HEADS] - log_total)

    def dot(a, b):
        return jnp.dot(a, b, preferred_element_type=F32)

    rs = []
    far = pl.ds((1 - y) * n_z, n_z)
    near = pl.ds(y * n_z, n_z)

    def part_cols(part):
        return slice(part * WIDE, (part + 1) * WIDE)

    def dq_step(part):
        for i in range(PER):
            h = part * PER + i
            probs = e_s[h] * factor[h : h + 1]
            dscore = (probs * (dp_s[h] - delta[h : h + 1])).astype(BF16)
            p_s[h] = probs.astype(BF16)
            ds_s[h] = dscore
            dq = lax.dot_general(dscore, k_ref[:, cols(h)], TN, preferred_element_type=F32) * SCALE
            dq = dq.reshape(2, 2 * n_z, rows, HD)
            dq_s[part, :, :, :, cols(i)] = dq
            dq_out[part, :, :, :, cols(i)] = dq.astype(BF16)
        rs.append(
            remote(dq_out.at[part, 1 - core], rs_c.at[part], rs_send.at[part, 0], rs_recv.at[part, 0], to_core)
        )

    def y_step(part):
        landed(rs_c.at[part], rs_send.at[part, 0], rs_recv.at[part, 0])
        y_out[part] = (dq_s[part, core, far] + rs_c[part, far].astype(F32)).astype(BF16)
        rs.append(remote(y_out.at[part], rs_y.at[part], rs_send.at[part, 1], rs_recv.at[part, 1], to_y))
        acc_s[part] = dq_s[part, core, near] + rs_c[part, near].astype(F32)

    def z_step(part):
        landed(rs_y.at[part], rs_send.at[part, 1], rs_recv.at[part, 1])
        acc = acc_s[part] + rs_y[part].astype(F32)
        acc_s[part] = acc
        z_out[part] = acc.astype(BF16)
        for j, o in enumerate(others_z):
            rs.append(
                remote(
                    z_out.at[part, o], rs_z.at[part, z], rs_send.at[part, 2 + j], rs_recv.at[part, 2 + z],
                    dev(o, y, core),
                )
            )

    def grad_v(h):
        gv_ref[:, cols(h)] = dot(p_s[h], head_of(do_all, h)).astype(BF16)

    def grad_k(h):
        gk_ref[:, cols(h)] = (dot(ds_s[h], head_of(q_all, h)) * SCALE).astype(BF16)

    dq_step(0)
    dq_step(1)
    y_step(0)
    dq_step(2)
    y_step(1)
    z_step(0)
    y_step(2)

    null_s[0, :HEADS, :] = null_ds
    null_s[1, :HEADS, :] = null_prob
    null_s[:, HEADS:, :] = jnp.zeros((2, 16 - HEADS, qt), F32)
    ds_high, ds_low = halves(null_s[0])
    p_high, p_low = halves(null_s[1])

    sum_k = jnp.where(diagonal, dot(ds_high, whole_q) + dot(ds_low, whole_q), 0.0) * SCALE
    sum_v = jnp.where(diagonal, dot(p_high, whole_do) + dot(p_low, whole_do), 0.0)
    null_sums[clip, 0:1, :] = jnp.sum(sum_k, axis=0, keepdims=True)
    null_sums[clip, 1:2, :] = jnp.sum(sum_v, axis=0, keepdims=True)
    ns = [
        remote(null_sums.at[clip], null_sums.at[clip], n_send.at[j], n_recv.at[clip], (o, bank))
        for j, o in enumerate(clip_peers)
    ]
    z_step(1)
    for h in range(HEADS // 2):
        grad_v(h)
    z_step(2)
    for h in range(HEADS // 2, HEADS):
        grad_v(h)
    stores = [pltpu.make_async_copy(gv_ref, gv_hbm, load_sem.at[6])]
    stores[0].start()

    own_at = lax.broadcasted_iota(jnp.int32, (rows, qt), 1) - mine * rows
    pick = (own_at == lax.broadcasted_iota(jnp.int32, (rows, qt), 0)).astype(F32).astype(BF16)
    own_high = nt_dot(pick, ds_high).astype(BF16)
    own_low = nt_dot(pick, ds_low).astype(BF16)
    null_term = (dot(own_high, nk_diag) + dot(own_low, nk_diag)) * SCALE
    for h in range(HEADS):
        grad_k(h)
    stores.append(pltpu.make_async_copy(gk_ref, gk_hbm, load_sem.at[7]))
    stores[1].start()

    for part in range(PARTS):
        total = acc_s[part, z] + null_term[:, part_cols(part)]
        for o in others_z:
            landed(rs_z.at[part, o], rs_send.at[part, 2], rs_recv.at[part, 2 + o])
            total = total + rs_z[part, o].astype(F32)
        gq_ref[:, part_cols(part)] = total.astype(BF16)
    for o in clip_peers:
        landed(null_sums.at[o], n_send.at[0], n_recv.at[o])
    both = null_sums[0]
    for i in range(1, n_clip):
        both = both + null_sums[i]
    gn_ref[...] = both
    for copy in sends + st + rs + ns:
        copy.wait_send()
    for store in stores:
        store.wait()


def write_out(gq, gk, gv, gn, gq_out, gk_out, gv_out, gnk_out, gnv_out):
    gq_out[...] = gq[...]
    gk_out[...] = gk[...]
    gv_out[...] = gv[...]
    gnk_out[...] = gn[0]
    gnv_out[...] = gn[1]


def on_device(n_clip, n_bank, queries, keys, values, grad_out, null_key, null_value, bank_counts, block_slot):
    own_rows = queries.shape[1]
    rows = -(-own_rows // 16) * 16
    blk = keys.shape[1]
    q, do = queries[0], grad_out[0]
    if rows != own_rows:
        q = jnp.pad(q, ((0, rows - own_rows), (0, 0)))
        do = jnp.pad(do, ((0, rows - own_rows), (0, 0)))
    n_z = n_bank // 4
    qt = n_bank * rows
    valid = jnp.clip(bank_counts[0] - block_slot * blk, 0, blk)
    vmem = pl.BlockSpec(memory_space=pltpu.VMEM)
    hbm = pl.BlockSpec(memory_space=pltpu.HBM)
    dma = pltpu.SemaphoreType.DMA
    shapes = (
        jax.ShapeDtypeStruct((rows, HW), BF16),
        jax.ShapeDtypeStruct((blk, HW), BF16),
        jax.ShapeDtypeStruct((blk, HW), BF16),
    )
    made = pl.pallas_call(
        functools.partial(kernel, n_clip, n_z, rows, blk),
        out_shape=shapes + (jax.ShapeDtypeStruct((2, HW), F32),),
        in_specs=[pl.BlockSpec(memory_space=pltpu.SMEM)] + [hbm] * 6,
        out_specs=[vmem, hbm, hbm, vmem],
        scratch_shapes=[
            pltpu.VMEM((n_bank, rows, HW), BF16),
            pltpu.VMEM((n_bank, rows, HW), BF16),
            pltpu.VMEM((HEADS, blk, qt), F32),
            pltpu.VMEM((HEADS, blk, qt), F32),
            pltpu.VMEM((HEADS, blk, qt), BF16),
            pltpu.VMEM((HEADS, blk, qt), BF16),
            pltpu.VMEM((PARTS, 2, 2 * n_z, rows, WIDE), F32),
            pltpu.VMEM((PARTS, 2, 2 * n_z, rows, WIDE), BF16),
            pltpu.VMEM((PARTS, 2 * n_z, rows, WIDE), BF16),
            pltpu.VMEM((PARTS, n_z, rows, WIDE), BF16),
            pltpu.VMEM((PARTS, n_z, rows, WIDE), BF16),
            pltpu.VMEM((PARTS, n_z, rows, WIDE), F32),
            pltpu.VMEM((PARTS, n_z, rows, WIDE), BF16),
            pltpu.VMEM((PARTS, n_z, rows, WIDE), BF16),
            pltpu.VMEM((16, qt), F32),
            pltpu.VMEM((4, 2 * HEADS, qt), F32),
            pltpu.VMEM((n_z, 2 * HEADS, qt), F32),
            pltpu.VMEM((2, 16, qt), F32),
            pltpu.VMEM((n_clip, 2, HW), F32),
            pltpu.VMEM((blk, HW), BF16),
            pltpu.VMEM((blk, HW), BF16),
            pltpu.VMEM((HW,), BF16),
            pltpu.VMEM((HW,), BF16),
            pltpu.VMEM((blk, HW), BF16),
            pltpu.VMEM((blk, HW), BF16),
            dma((8,)),
            dma((2, n_bank)),
            dma((2, 2)),
            dma((2, n_z)),
            dma((2, n_z)),
            dma((2, 2)),
            dma((2, max(4, n_z))),
            dma((2, max(4, n_z))),
            dma((PARTS, 2 + n_z)),
            dma((PARTS, 2 + n_z)),
            dma((n_clip,)),
            dma((n_clip,)),
        ],
        compiler_params=pltpu.CompilerParams(
            collective_id=0, has_side_effects=True, vmem_limit_bytes=58 * 1024 * 1024
        ),
    )(valid, q, keys[0], values[0], do, null_key, null_value)
    vector = jax.ShapeDtypeStruct((HW,), F32)
    gq, gk, gv, gnk, gnv = pl.pallas_call(
        write_out,
        out_shape=shapes + (vector, vector),
        in_specs=[vmem] * 4,
        out_specs=[vmem] * 5,
        compiler_params=pltpu.CompilerParams(vmem_limit_bytes=60 * 1024 * 1024),
    )(*made)
    return gq[None, :own_rows], gk[None], gv[None], gnk, gnv


def solution(mesh):
    return jax.shard_map(
        functools.partial(on_device, mesh.shape["clip"], mesh.shape["bank"]),
        mesh=mesh,
        in_specs=(
            P("clip", "bank", None),
            P("clip", "bank", None),
            P("clip", "bank", None),
            P("clip", "bank", None),
            P(),
            P(),
            P("clip"),
            P("clip", "bank"),
        ),
        out_specs=(
            P("clip", "bank", None),
            P("clip", "bank", None),
            P("clip", "bank", None),
            P(),
            P(),
        ),
        check_vma=False,
    )
```

profile of v0, /device:TPU:0, one launch (start us, length us, event | category | flops | bytes accessed | tf_op | source)
XLA Modules:
  0.0 49.2 jit_solution(7124160372950068825)
XLA Ops:
  1.9 45.2 %shard_map.119 = (bf16[16,1536]{1,0:T(8,128)(2,1)}, bf16[128,1536]{1,0:T(8,128)(2,1)}, bf16[128,1536]{1,0:T(8,128)(2,1)}, f32[2,1536]{1,0:T(2,128)}) custom-call(s32[1,1]{1,0:T(1,128)S(6)} %min.6.valid_ref, bf16[16,1536]{1,0:T(8,128)(2,1)} %bitcast.11, bf16[128,1536]{1,0:T(8,128)(2,1)} %bitcast.9, bf16[128,1536]{1,0:T(8,128)(2,1)} %bitcast.10, ...), custom_call_target="tpu_custom_call" | custom-call | tf_op jit(solution)/shard_map/pallas_call | solution.py:357
  47.1 2.1 %shard_map.120 = (bf16[16,1536]{1,0:T(8,128)(2,1)}, bf16[128,1536]{1,0:T(8,128)(2,1)}, bf16[128,1536]{1,0:T(8,128)(2,1)}, f32[1536]{0:T(1024)}, f32[1536]{0:T(1024)}) custom-call(bf16[16,1536]{1,0:T(8,128)(2,1)} %get-tuple-element.14.gq, bf16[128,1536]{1,0:T(8,128)(2,1)} %get-tuple-element.15.gk, bf16[128,1536]{1,0:T(8,128)(2,1)} %get-tuple-element.16.gv, ...), custom_call_target="tpu_custom_call" | custom-call | tf_op jit(solution)/shard_map/pallas_call | solution.py:406
where the time goes:
time: 49.4 us; the launch traced here: 49.2 us
  Pallas kernels  47.3 us (96%)
  between operations  1.94 us (4%)
    pallas_call x1, Pallas kernels, on_device(): pl.pallas_call(functools.partial(kernel, n_clip, n_z, rows, blk), out_sha...  45.2 us
    pallas_call x1, Pallas kernels, on_device(): pl.pallas_call(write_out, out_shape=shapes + (vector, vector), in_specs=[...  2.07 us

commit v1 on v0

--- a/solution.py
+++ b/solution.py
@@ -41,8 +41,8 @@
 
 def kernel(
     n_clip, n_z, rows, blk,
-    valid_ref, q_hbm, k_hbm, v_hbm, do_hbm, nk_hbm, nv_hbm,
-    gq_ref, gk_hbm, gv_hbm, gn_ref,
+    count_ref, slot_ref, q_hbm, k_hbm, v_hbm, do_hbm, nk_hbm, nv_hbm,
+    gq_ref, gk_hbm, gv_hbm, gnk_ref, gnv_ref,
     q_all, do_all, e_s, dp_s, p_s, ds_s, dq_s, dq_out, rs_c, y_out, rs_y, acc_s, z_out, rs_z,
     peak_s, st_lo, st_z, null_s, null_sums,
     k_ref, v_ref, nk_ref, nv_ref, gk_ref, gv_ref, load_sem,
@@ -145,7 +145,7 @@
     loads[2].wait()
     from_core(0)
 
-    live = lax.broadcasted_iota(jnp.int32, (blk, qt), 0) < valid_ref[0, 0]
+    live = lax.broadcasted_iota(jnp.int32, (blk, qt), 0) < count_ref[0] - slot_ref[0, 0] * blk
     lo = core * 2 + y
 
     def cols(h):
@@ -235,7 +235,7 @@
             dscore = (probs * (dp_s[h] - delta[h : h + 1])).astype(BF16)
             p_s[h] = probs.astype(BF16)
             ds_s[h] = dscore
-            dq = lax.dot_general(dscore, k_ref[:, cols(h)], TN, preferred_element_type=F32) * SCALE
+            dq = lax.dot_general(dscore, k_ref[:, cols(h)], TN, preferred_element_type=F32)
             dq = dq.reshape(2, 2 * n_z, rows, HD)
             dq_s[part, :, :, :, cols(i)] = dq
             dq_out[part, :, :, :, cols(i)] = dq.astype(BF16)
@@ -282,8 +282,10 @@
     ds_high, ds_low = halves(null_s[0])
     p_high, p_low = halves(null_s[1])
 
-    sum_k = jnp.where(diagonal, dot(ds_high, whole_q) + dot(ds_low, whole_q), 0.0) * SCALE
-    sum_v = jnp.where(diagonal, dot(p_high, whole_do) + dot(p_low, whole_do), 0.0)
+    sum_k = dot(jnp.concatenate([ds_high, ds_low], axis=0), whole_q)
+    sum_k = jnp.where(diagonal, sum_k[:16] + sum_k[16:], 0.0) * SCALE
+    sum_v = dot(jnp.concatenate([p_high, p_low], axis=0), whole_do)
+    sum_v = jnp.where(diagonal, sum_v[:16] + sum_v[16:], 0.0)
     null_sums[clip, 0:1, :] = jnp.sum(sum_k, axis=0, keepdims=True)
     null_sums[clip, 1:2, :] = jnp.sum(sum_v, axis=0, keepdims=True)
     ns = [
@@ -303,36 +305,38 @@
     pick = (own_at == lax.broadcasted_iota(jnp.int32, (rows, qt), 0)).astype(F32).astype(BF16)
     own_high = nt_dot(pick, ds_high).astype(BF16)
     own_low = nt_dot(pick, ds_low).astype(BF16)
-    null_term = (dot(own_high, nk_diag) + dot(own_low, nk_diag)) * SCALE
+    null_term = dot(own_high, nk_diag) + dot(own_low, nk_diag)
     for h in range(HEADS):
         grad_k(h)
     stores.append(pltpu.make_async_copy(gk_ref, gk_hbm, load_sem.at[7]))
     stores[1].start()
 
     for part in range(PARTS):
-        total = acc_s[part, z] + null_term[:, part_cols(part)]
+        total = acc_s[part, z]
         for o in others_z:
             landed(rs_z.at[part, o], rs_send.at[part, 2], rs_recv.at[part, 2 + o])
             total = total + rs_z[part, o].astype(F32)
-        gq_ref[:, part_cols(part)] = total.astype(BF16)
+        gq_ref[:, part_cols(part)] = ((total + null_term[:, part_cols(part)]) * SCALE).astype(BF16)
     for o in clip_peers:
         landed(null_sums.at[o], n_send.at[0], n_recv.at[o])
     both = null_sums[0]
     for i in range(1, n_clip):
         both = both + null_sums[i]
-    gn_ref[...] = both
+    gnk_ref[...] = both[0]
+    gnv_ref[...] = both[1]
     for copy in sends + st + rs + ns:
         copy.wait_send()
     for store in stores:
         store.wait()
 
 
-def write_out(gq, gk, gv, gn, gq_out, gk_out, gv_out, gnk_out, gnv_out):
-    gq_out[...] = gq[...]
-    gk_out[...] = gk[...]
-    gv_out[...] = gv[...]
-    gnk_out[...] = gn[0]
-    gnv_out[...] = gn[1]
+def write_out(*refs):
+    made, outs, sems = refs[:5], refs[5:10], refs[10]
+    copies = [pltpu.make_async_copy(src, dst, sems.at[i]) for i, (src, dst) in enumerate(zip(made, outs))]
+    for copy in copies:
+        copy.start()
+    for copy in copies:
+        copy.wait()
 
 
 def on_device(n_clip, n_bank, queries, keys, values, grad_out, null_key, null_value, bank_counts, block_slot):
@@ -345,7 +349,6 @@
         do = jnp.pad(do, ((0, rows - own_rows), (0, 0)))
     n_z = n_bank // 4
     qt = n_bank * rows
-    valid = jnp.clip(bank_counts[0] - block_slot * blk, 0, blk)
     vmem = pl.BlockSpec(memory_space=pltpu.VMEM)
     hbm = pl.BlockSpec(memory_space=pltpu.HBM)
     dma = pltpu.SemaphoreType.DMA
@@ -354,11 +357,12 @@
         jax.ShapeDtypeStruct((blk, HW), BF16),
         jax.ShapeDtypeStruct((blk, HW), BF16),
     )
+    vector = jax.ShapeDtypeStruct((HW,), F32)
     made = pl.pallas_call(
         functools.partial(kernel, n_clip, n_z, rows, blk),
-        out_shape=shapes + (jax.ShapeDtypeStruct((2, HW), F32),),
-        in_specs=[pl.BlockSpec(memory_space=pltpu.SMEM)] + [hbm] * 6,
-        out_specs=[vmem, hbm, hbm, vmem],
+        out_shape=shapes + (vector, vector),
+        in_specs=[pl.BlockSpec(memory_space=pltpu.SMEM)] * 2 + [hbm] * 6,
+        out_specs=[vmem, hbm, hbm, vmem, vmem],
         scratch_shapes=[
             pltpu.VMEM((n_bank, rows, HW), BF16),
             pltpu.VMEM((n_bank, rows, HW), BF16),
@@ -401,13 +405,13 @@
         compiler_params=pltpu.CompilerParams(
             collective_id=0, has_side_effects=True, vmem_limit_bytes=58 * 1024 * 1024
         ),
-    )(valid, q, keys[0], values[0], do, null_key, null_value)
-    vector = jax.ShapeDtypeStruct((HW,), F32)
+    )(bank_counts, block_slot, q, keys[0], values[0], do, null_key, null_value)
     gq, gk, gv, gnk, gnv = pl.pallas_call(
         write_out,
         out_shape=shapes + (vector, vector),
-        in_specs=[vmem] * 4,
-        out_specs=[vmem] * 5,
+        in_specs=[hbm] * 5,
+        out_specs=[hbm] * 5,
+        scratch_shapes=[dma((5,))],
         compiler_params=pltpu.CompilerParams(vmem_limit_bytes=60 * 1024 * 1024),
     )(*made)
     return gq[None, :own_rows], gk[None], gv[None], gnk, gnv

time: 49.4 us -> 74.2 us (1.50)
  Pallas kernels: 47.3 us -> 72.1 us
    pallas_call x1, Pallas kernels: 2.07 us -> 26.8 us  [on_device(): pl.pallas_call(write_out, out_shape=shapes + (vector, vector), in_specs=[...]
where the time goes in v1:
time: 74.2 us; the launch traced here: 74 us
  Pallas kernels  72.1 us (97%)
  between operations  1.93 us (3%)
    pallas_call x1, Pallas kernels, on_device(): pl.pallas_call(functools.partial(kernel, n_clip, n_z, rows, blk), out_sha...  45.2 us
    pallas_call x1, Pallas kernels, on_device(): pl.pallas_call(write_out, out_shape=shapes + (vector, vector), in_specs=[...  26.8 us

profile of v1, /device:TPU:0, one launch (start us, length us, event | category | flops | bytes accessed | tf_op | source)
XLA Modules:
  0.0 74.0 jit_solution(13235905551326621488)
XLA Ops:
  1.9 45.2 %shard_map.119 = (bf16[16,1536]{1,0:T(8,128)(2,1)}, bf16[128,1536]{1,0:T(8,128)(2,1)}, bf16[128,1536]{1,0:T(8,128)(2,1)}, f32[1536]{0:T(1024)}, f32[1536]{0:T(1024)}) custom-call(s32[1]{0:T(128)S(6)} %copy.13.count_ref, s32[1,1]{1,0:T(1,128)S(6)} %copy.14.slot_ref, bf16[16,1536]{1,0:T(8,128)(2,1)} %bitcast.9, bf16[128,1536]{1,0:T(8,128)(2,1)} %bitcast.7, ...), custom_call_target="tpu_custom_call" | custom-call | tf_op jit(solution)/shard_map/pallas_call | solution.py:361
  47.2 26.8 %shard_map.120 = (bf16[16,1536]{1,0:T(8,128)(2,1)}, bf16[128,1536]{1,0:T(8,128)(2,1)}, bf16[128,1536]{1,0:T(8,128)(2,1)}, f32[1536]{0:T(1024)}, f32[1536]{0:T(1024)}) custom-call(bf16[16,1536]{1,0:T(8,128)(2,1)} %get-tuple-element.15.refs_0_, bf16[128,1536]{1,0:T(8,128)(2,1)} %get-tuple-element.16.refs_1_, bf16[128,1536]{1,0:T(8,128)(2,1)} %get-tuple-element.17.refs_2_, ...), custom_call_target="tpu_custom_call" | custom-call | tf_op jit(solution)/shard_map/pallas_call | solution.py:409

commit v2 on v1

--- a/solution.py
+++ b/solution.py
@@ -138,9 +138,11 @@
     loads[0].wait()
     own_sends(0)
     loads[1].wait()
+    steps = 2 * n_z - 1
+    for step in range(n_z - 1):
+        forward(0, step)
     own_sends(1)
-    steps = 2 * n_z - 1
-    for step in range(steps):
+    for step in range(n_z - 1, steps):
         forward(0, step)
     loads[2].wait()
     from_core(0)
@@ -331,12 +333,16 @@
 
 
 def write_out(*refs):
-    made, outs, sems = refs[:5], refs[5:10], refs[10]
-    copies = [pltpu.make_async_copy(src, dst, sems.at[i]) for i, (src, dst) in enumerate(zip(made, outs))]
-    for copy in copies:
-        copy.start()
-    for copy in copies:
-        copy.wait()
+    made, outs, held, load_sems, store_sems = refs[:5], refs[5:10], refs[10:15], refs[15], refs[16]
+    loads = [pltpu.make_async_copy(src, at, load_sems.at[i]) for i, (src, at) in enumerate(zip(made, held))]
+    stores = [pltpu.make_async_copy(at, dst, store_sems.at[i]) for i, (at, dst) in enumerate(zip(held, outs))]
+    for load in loads:
+        load.start()
+    for load, store in zip(loads, stores):
+        load.wait()
+        store.start()
+    for store in stores:
+        store.wait()
 
 
 def on_device(n_clip, n_bank, queries, keys, values, grad_out, null_key, null_value, bank_counts, block_slot):
@@ -411,7 +417,7 @@
         out_shape=shapes + (vector, vector),
         in_specs=[hbm] * 5,
         out_specs=[hbm] * 5,
-        scratch_shapes=[dma((5,))],
+        scratch_shapes=[pltpu.VMEM(one.shape, one.dtype) for one in shapes + (vector, vector)] + [dma((5,)), dma((5,))],
         compiler_params=pltpu.CompilerParams(vmem_limit_bytes=60 * 1024 * 1024),
     )(*made)
     return gq[None, :own_rows], gk[None], gv[None], gnk, gnv

time: 74.2 us -> 47.6 us (0.64)
  Pallas kernels: 72.1 us -> 45.5 us
    pallas_call x1, Pallas kernels: 26.8 us -> 1.99 us  [on_device(): pl.pallas_call(write_out, out_shape=shapes + (vector, vector), in_specs=[...]
    pallas_call x1, Pallas kernels: 45.2 us -> 43.5 us  [on_device(): pl.pallas_call(functools.partial(kernel, n_clip, n_z, rows, blk), out_sha...]
where the time goes in v2:
time: 47.6 us; the launch traced here: 47.4 us
  Pallas kernels  45.5 us (96%)
  between operations  1.93 us (4%)
    pallas_call x1, Pallas kernels, on_device(): pl.pallas_call(functools.partial(kernel, n_clip, n_z, rows, blk), out_sha...  43.5 us
    pallas_call x1, Pallas kernels, on_device(): pl.pallas_call(write_out, out_shape=shapes + (vector, vector), in_specs=[...  1.99 us

profile of v2, /device:TPU:0, one launch (start us, length us, event | category | flops | bytes accessed | tf_op | source)
XLA Modules:
  0.0 47.4 jit_solution(11910424954988911739)
XLA Ops:
  1.9 43.5 %shard_map.119 = (bf16[16,1536]{1,0:T(8,128)(2,1)}, bf16[128,1536]{1,0:T(8,128)(2,1)}, bf16[128,1536]{1,0:T(8,128)(2,1)}, f32[1536]{0:T(1024)}, f32[1536]{0:T(1024)}) custom-call(s32[1]{0:T(128)S(6)} %copy.13.count_ref, s32[1,1]{1,0:T(1,128)S(6)} %copy.14.slot_ref, bf16[16,1536]{1,0:T(8,128)(2,1)} %bitcast.9, bf16[128,1536]{1,0:T(8,128)(2,1)} %bitcast.7, ...), custom_call_target="tpu_custom_call" | custom-call | tf_op jit(solution)/shard_map/pallas_call | solution.py:367
  45.4 2.0 %shard_map.120 = (bf16[16,1536]{1,0:T(8,128)(2,1)}, bf16[128,1536]{1,0:T(8,128)(2,1)}, bf16[128,1536]{1,0:T(8,128)(2,1)}, f32[1536]{0:T(1024)}, f32[1536]{0:T(1024)}) custom-call(bf16[16,1536]{1,0:T(8,128)(2,1)} %get-tuple-element.15.refs_0_, bf16[128,1536]{1,0:T(8,128)(2,1)} %get-tuple-element.16.refs_1_, bf16[128,1536]{1,0:T(8,128)(2,1)} %get-tuple-element.17.refs_2_, ...), custom_call_target="tpu_custom_call" | custom-call | tf_op jit(solution)/shard_map/pallas_call | solution.py:415

commit v3 on v2

--- a/solution.py
+++ b/solution.py
@@ -170,21 +170,46 @@
         total = jnp.sum(e, axis=0, keepdims=True)
         e_s[h] = e
         peak_s[h : h + 1, :] = peak
-        st_lo[lo, h : h + 1, :] = peak + jnp.log(total)
+        st_lo[h // PER, lo, h % PER : h % PER + 1, :] = peak + jnp.log(total)
         totals.append(total)
     for step in range(done, steps):
         forward(1, step)
     loads[3].wait()
     from_core(1)
-    for h in range(HEADS):
-        dp = nt_dot(v_ref[:, cols(h)], head_of(do_all, h))
-        dp_s[h] = dp
-        st_lo[lo, HEADS + h : HEADS + h + 1, :] = jnp.sum(e_s[h] * dp, axis=0, keepdims=True) / totals[h]
-
-    st = [
-        remote(st_lo.at[lo], st_lo.at[lo], st_send.at[0, i], st_recv.at[0, lo], dev(z, a, b))
-        for i, (a, b) in enumerate(lo_peers)
-    ]
+    st = []
+
+    def delta_part(part):
+        for i in range(PER):
+            h = part * PER + i
+            dp = nt_dot(v_ref[:, cols(h)], head_of(do_all, h))
+            dp_s[h] = dp
+            delta = jnp.sum(e_s[h] * dp, axis=0, keepdims=True) / totals[h]
+            st_lo[part, lo, PER + i : PER + i + 1, :] = delta
+        own = st_lo.at[part, lo]
+        for i, (a, b) in enumerate(lo_peers):
+            st.append(remote(own, own, st_send.at[part, i], st_recv.at[part, lo], dev(z, a, b)))
+
+    def merged(buf, part, count):
+        return merge([buf[part, i, :PER] for i in range(count)], [buf[part, i, PER:] for i in range(count)])
+
+    def spread_part(part):
+        for a, b in lo_peers:
+            at = b * 2 + a
+            landed(st_lo.at[part, at], st_send.at[part, 0], st_recv.at[part, at])
+        lse, delta = merged(st_lo, part, 4)
+        st_z[part, z, :PER, :] = lse
+        st_z[part, z, PER:, :] = delta
+        own = st_z.at[part, z]
+        for j, o in enumerate(others_z):
+            st.append(
+                remote(own, own, st_send.at[PARTS + part, j], st_recv.at[PARTS + part, z], dev(o, y, core))
+            )
+
+    delta_part(0)
+    delta_part(1)
+    spread_part(0)
+    delta_part(2)
+    spread_part(1)
     loads[4].wait()
     loads[5].wait()
     row_of = lax.broadcasted_iota(jnp.int32, (16, HW), 0)
@@ -196,29 +221,21 @@
     whole_do = do_all[...].reshape(qt, HW)
     null_score = (nt_dot(nk_diag, whole_q) * SCALE)[:HEADS]
     null_dp = nt_dot(nv_diag, whole_do)[:HEADS]
-
-    def stat_arrived(stage, buf, at):
-        pltpu.make_async_remote_copy(
-            src_ref=buf.at[at], dst_ref=buf.at[at], send_sem=st_send.at[stage, 0], recv_sem=st_recv.at[stage, at],
-            device_id=to_core, device_id_type=pl.DeviceIdType.MESH,
-        ).wait_recv()
-
-    for a, b in lo_peers:
-        stat_arrived(0, st_lo, b * 2 + a)
-    lse, delta = merge([st_lo[i, :HEADS] for i in range(4)], [st_lo[i, HEADS:] for i in range(4)])
-    st_z[z, :HEADS, :] = lse
-    st_z[z, HEADS:, :] = delta
-    for j, o in enumerate(others_z):
-        st.append(remote(st_z.at[z], st_z.at[z], st_send.at[1, j], st_recv.at[1, z], dev(o, y, core)))
-    for o in others_z:
-        stat_arrived(1, st_z, o)
-    lse, delta = merge([st_z[i, :HEADS] for i in range(n_z)], [st_z[i, HEADS:] for i in range(n_z)])
-    top = jnp.maximum(lse, null_score)
-    log_total = top + jnp.log(jnp.exp(lse - top) + jnp.exp(null_score - top))
-    null_prob = jnp.exp(null_score - log_total)
-    delta = jnp.exp(lse - log_total) * delta + null_prob * null_dp
-    null_ds = null_prob * (null_dp - delta)
-    factor = jnp.exp(peak_s[:HEADS] - log_total)
+    spread_part(2)
+
+    def final_part(part):
+        for o in others_z:
+            landed(st_z.at[part, o], st_send.at[PARTS + part, 0], st_recv.at[PARTS + part, o])
+        lse, delta = merged(st_z, part, n_z)
+        at = slice(part * PER, (part + 1) * PER)
+        score, null_d = null_score[at], null_dp[at]
+        top = jnp.maximum(lse, score)
+        log_total = top + jnp.log(jnp.exp(lse - top) + jnp.exp(score - top))
+        null_prob = jnp.exp(score - log_total)
+        delta = jnp.exp(lse - log_total) * delta + null_prob * null_d
+        null_s[0, at, :] = null_prob * (null_d - delta)
+        null_s[1, at, :] = null_prob
+        return jnp.exp(peak_s[at] - log_total), delta
 
     def dot(a, b):
         return jnp.dot(a, b, preferred_element_type=F32)
@@ -231,10 +248,11 @@
         return slice(part * WIDE, (part + 1) * WIDE)
 
     def dq_step(part):
+        factor, delta = final_part(part)
         for i in range(PER):
             h = part * PER + i
-            probs = e_s[h] * factor[h : h + 1]
-            dscore = (probs * (dp_s[h] - delta[h : h + 1])).astype(BF16)
+            probs = e_s[h] * factor[i : i + 1]
+            dscore = (probs * (dp_s[h] - delta[i : i + 1])).astype(BF16)
             p_s[h] = probs.astype(BF16)
             ds_s[h] = dscore
             dq = lax.dot_general(dscore, k_ref[:, cols(h)], TN, preferred_element_type=F32)
@@ -278,8 +296,6 @@
     z_step(0)
     y_step(2)
 
-    null_s[0, :HEADS, :] = null_ds
-    null_s[1, :HEADS, :] = null_prob
     null_s[:, HEADS:, :] = jnp.zeros((2, 16 - HEADS, qt), F32)
     ds_high, ds_low = halves(null_s[0])
     p_high, p_low = halves(null_s[1])
@@ -385,8 +401,8 @@
             pltpu.VMEM((PARTS, n_z, rows, WIDE), BF16),
             pltpu.VMEM((PARTS, n_z, rows, WIDE), BF16),
             pltpu.VMEM((16, qt), F32),
-            pltpu.VMEM((4, 2 * HEADS, qt), F32),
-            pltpu.VMEM((n_z, 2 * HEADS, qt), F32),
+            pltpu.VMEM((PARTS, 4, 2 * PER, qt), F32),
+            pltpu.VMEM((PARTS, n_z, 2 * PER, qt), F32),
             pltpu.VMEM((2, 16, qt), F32),
             pltpu.VMEM((n_clip, 2, HW), F32),
             pltpu.VMEM((blk, HW), BF16),
@@ -401,8 +417,8 @@
             dma((2, n_z)),
             dma((2, n_z)),
             dma((2, 2)),
-            dma((2, max(4, n_z))),
-            dma((2, max(4, n_z))),
+            dma((2 * PARTS, max(4, n_z))),
+            dma((2 * PARTS, max(4, n_z))),
             dma((PARTS, 2 + n_z)),
             dma((PARTS, 2 + n_z)),
             dma((n_clip,)),

time: 47.6 us -> 46.2 us (0.971)
  Pallas kernels: 45.5 us -> 44.1 us
    pallas_call x1, Pallas kernels: 43.5 us -> 42.1 us  [on_device(): pl.pallas_call(functools.partial(kernel, n_clip, n_z, rows, blk), out_sha...]
where the time goes in v3:
time: 46.2 us; the launch traced here: 46 us
  Pallas kernels  44.1 us (95%)
  between operations  1.93 us (4%)
    pallas_call x1, Pallas kernels, on_device(): pl.pallas_call(functools.partial(kernel, n_clip, n_z, rows, blk), out_sha...  42.1 us
    pallas_call x1, Pallas kernels, on_device(): pl.pallas_call(write_out, out_shape=shapes + (vector, vector), in_specs=[...  1.99 us

profile of v3, /device:TPU:0, one launch (start us, length us, event | category | flops | bytes accessed | tf_op | source)
XLA Modules:
  0.0 46.0 jit_solution(16700808792599479396)
XLA Ops:
  1.9 42.1 %shard_map.119 = (bf16[16,1536]{1,0:T(8,128)(2,1)}, bf16[128,1536]{1,0:T(8,128)(2,1)}, bf16[128,1536]{1,0:T(8,128)(2,1)}, f32[1536]{0:T(1024)}, f32[1536]{0:T(1024)}) custom-call(s32[1]{0:T(128)S(6)} %copy.13.count_ref, s32[1,1]{1,0:T(1,128)S(6)} %copy.14.slot_ref, bf16[16,1536]{1,0:T(8,128)(2,1)} %bitcast.9, bf16[128,1536]{1,0:T(8,128)(2,1)} %bitcast.7, ...), custom_call_target="tpu_custom_call" | custom-call | tf_op jit(solution)/shard_map/pallas_call | solution.py:383
  44.1 2.0 %shard_map.120 = (bf16[16,1536]{1,0:T(8,128)(2,1)}, bf16[128,1536]{1,0:T(8,128)(2,1)}, bf16[128,1536]{1,0:T(8,128)(2,1)}, f32[1536]{0:T(1024)}, f32[1536]{0:T(1024)}) custom-call(bf16[16,1536]{1,0:T(8,128)(2,1)} %get-tuple-element.15.refs_0_, bf16[128,1536]{1,0:T(8,128)(2,1)} %get-tuple-element.16.refs_1_, bf16[128,1536]{1,0:T(8,128)(2,1)} %get-tuple-element.17.refs_2_, ...), custom_call_target="tpu_custom_call" | custom-call | tf_op jit(solution)/shard_map/pallas_call | solution.py:431

commit v4 on v3

--- a/solution.py
+++ b/solution.py
@@ -100,9 +100,9 @@
 
     def own_sends(a):
         own = gathered[a].at[mine]
+        sends.append(remote(own, own, g_send_y.at[a, 0], g_recv.at[a, mine], to_y))
         for j, o in enumerate(others_z):
             sends.append(remote(own, own, g_send_z.at[a, j], g_recv.at[a, mine], dev(o, y, core)))
-        sends.append(remote(own, own, g_send_y.at[a, 0], g_recv.at[a, mine], to_y))
 
     def landed(buf, send, recv):
         pltpu.make_async_remote_copy(

time: 46.2 us -> 46.2 us (level)
  no operation moved by 1% of the time
where the time goes in v4:
time: 46.2 us; the launch traced here: 46.1 us
  Pallas kernels  44.1 us (95%)
  between operations  1.93 us (4%)
    pallas_call x1, Pallas kernels, on_device(): pl.pallas_call(functools.partial(kernel, n_clip, n_z, rows, blk), out_sha...  42.1 us
    pallas_call x1, Pallas kernels, on_device(): pl.pallas_call(write_out, out_shape=shapes + (vector, vector), in_specs=[...  1.99 us

profile of v4, /device:TPU:0, one launch (start us, length us, event | category | flops | bytes accessed | tf_op | source)
XLA Modules:
  0.0 46.1 jit_solution(12990327308429187132)
XLA Ops:
  1.9 42.1 %shard_map.119 = (bf16[16,1536]{1,0:T(8,128)(2,1)}, bf16[128,1536]{1,0:T(8,128)(2,1)}, bf16[128,1536]{1,0:T(8,128)(2,1)}, f32[1536]{0:T(1024)}, f32[1536]{0:T(1024)}) custom-call(s32[1]{0:T(128)S(6)} %copy.13.count_ref, s32[1,1]{1,0:T(1,128)S(6)} %copy.14.slot_ref, bf16[16,1536]{1,0:T(8,128)(2,1)} %bitcast.9, bf16[128,1536]{1,0:T(8,128)(2,1)} %bitcast.7, ...), custom_call_target="tpu_custom_call" | custom-call | tf_op jit(solution)/shard_map/pallas_call | solution.py:383
  44.1 2.0 %shard_map.120 = (bf16[16,1536]{1,0:T(8,128)(2,1)}, bf16[128,1536]{1,0:T(8,128)(2,1)}, bf16[128,1536]{1,0:T(8,128)(2,1)}, f32[1536]{0:T(1024)}, f32[1536]{0:T(1024)}) custom-call(bf16[16,1536]{1,0:T(8,128)(2,1)} %get-tuple-element.15.refs_0_, bf16[128,1536]{1,0:T(8,128)(2,1)} %get-tuple-element.16.refs_1_, bf16[128,1536]{1,0:T(8,128)(2,1)} %get-tuple-element.17.refs_2_, ...), custom_call_target="tpu_custom_call" | custom-call | tf_op jit(solution)/shard_map/pallas_call | solution.py:431
